TPU v7x, 256 devices: a whole 4x4x8 slice. The times are simulated.
256 devices in a mesh: grp: 8 (over y, z_lo), row: 32 (over z_hi, x, core).
Axes of the slice: x: 4, y: 4, z: 8 (z_hi: 4, z_lo: 2; z = z_hi * 2 + z_lo), core: 2. Of those that a mesh axis runs over, the one named last changes fastest.
Arguments:
- matrix: float32 [1048576, 256], P(('grp', 'row')), may hold values from -6 to 6
- row_signs: int32 [1048576], P(('grp', 'row')), may hold values from -1 to 1, as said below
- block_dest: int32 [8192], P(('grp', 'row')), may hold values from 0 to 15
- block_signs: int32 [8192], P(('grp', 'row')), may hold values from -1 to 1, as said below
Outputs:
- sketch: float32 [2048, 256], P('row')
Inputs may be any that keep to these rules, and one draw needn't show every extreme that they name: `row_signs`: each entry is -1 or 1. `block_signs`: each entry is -1 or 1.
All inputs are finite; a program needn't handle non-finite values.
Results may differ from a plain program's by a relative error of at most 0.0003.
Values sent between devices are 32-bit elements; how exact they have to be, the bound alone decides.
No kernel may reach another device: no remote copies, remote signals or barrier semaphores. Data moves between devices by JAX's collectives and lax.ppermute only.
A program may use at most 64 MiB of HBM per device.

v0:
```python
import math
import jax
import jax.numpy as jnp
from jax import lax
from jax.sharding import PartitionSpec as P

SKETCH = 2048


def swapped(array, axis, stride):
    return lax.ppermute(array, axis, [(i, i ^ 1 << stride) for i in range(lax.axis_size(axis))])


def sylvester(order):
    indices = jnp.arange(order, dtype=jnp.int32)
    common = indices[:, None] & indices[None, :]
    parity = jnp.zeros((order, order), jnp.int32)
    for section in range(order.bit_length() - 1):
        parity = parity + (common >> section & 1)
    return (1 - 2 * (parity % 2)).astype(jnp.float32)


def unit_weights(dests, signs, start, piece, block, target_count):
    unit_rows = min(piece, block)
    unit_count = piece // unit_rows
    starts = start + jnp.arange(unit_count, dtype=jnp.int32) * unit_rows
    which_block = starts // block
    offset = starts % block // unit_rows
    dest_sel = jnp.take(dests, which_block, axis=1)
    sign_sel = jnp.take(signs, which_block, axis=1).astype(jnp.float32)
    targets = jnp.arange(target_count, dtype=jnp.int32)
    within = jnp.arange(block // unit_rows, dtype=jnp.int32)
    to_dest = (dest_sel[None, :, :] == targets[:, None, None]).astype(jnp.float32) * sign_sel[
        None, :, :
    ]
    to_slot = (offset[None, :] == within[:, None]).astype(jnp.float32)
    return to_dest[:, None, :, :] * to_slot[None, :, None, :]


def place(weights, held, block):
    sources, piece, columns = held.shape
    unit_rows = min(piece, block)
    grid = held.reshape(sources, piece // unit_rows, unit_rows, columns)
    return jnp.einsum("sjmk,mkuc->sjuc", weights, grid, precision=lax.Precision.HIGHEST)


def body(matrix, row_signs, block_dest, block_signs):
    precise = lax.Precision.HIGHEST
    row_count, col_count = matrix.shape
    block = row_count // block_dest.shape[0]
    target_count = SKETCH // block
    dev_count = lax.axis_size("row")
    my_index = lax.axis_index("row")
    exponent = row_count.bit_length() - 1
    first_size = 1 << exponent // 2
    second_size = row_count // first_size
    signed = matrix * row_signs[:, None].astype(jnp.float32)
    shaped = signed.reshape(first_size, second_size, col_count)
    shaped = jnp.einsum("ya,abc->ybc", sylvester(first_size), shaped, precision=precise)
    shaped = jnp.einsum("zb,abc->azc", sylvester(second_size), shaped, precision=precise)
    mixed = shaped.reshape(row_count, col_count) / math.sqrt(row_count)
    flipped = mixed
    inverse_root = 1.0 / math.sqrt(2.0)
    for section in range(dev_count.bit_length() - 1):
        partner = swapped(flipped, "row", section)
        upper = my_index >> section & 1 == 1
        flipped = jnp.where(upper, partner - flipped, flipped + partner) * inverse_root
    weights = unit_weights(
        block_dest[None, :], block_signs[None, :], 0, row_count, block, target_count
    )
    partial_value = place(weights, flipped[None, :, :], block)
    partial_value = partial_value.reshape(SKETCH, col_count)
    group_count = lax.axis_size("grp")
    share = lax.psum_scatter(partial_value, "row", scatter_dimension=0, tiled=True)
    summed = lax.psum(share, "grp")
    total_rows = row_count * dev_count * group_count
    return summed * math.sqrt(SKETCH / total_rows)


def solution(mesh):
    return jax.shard_map(
        body,
        mesh=mesh,
        in_specs=(P(("grp", "row"), None), P(("grp", "row")), P(("grp", "row")), P(("grp", "row"))),
        out_specs=P("row", None),
        check_vma=False,
    )
```

profile of v0, /device:TPU:2, one launch (start us, length us, event | category | flops | bytes accessed | tf_op | source)
XLA Modules:
  0.0 799.0 jit_solution(16415899795226942938)
XLA Ops:
  6.5 0.7 convert_element_type.29
  7.3 2.6 broadcast_multiply_fusion
  9.9 6.3 fusion.2
  16.1 7.1 fusion.6
  23.3 7.5 collective-permute-done
  30.8 5.9 select_multiply_fusion.4
  36.7 2.3 collective-permute-start.1
  39.0 91.2 %collective-permute-done.1 = f32[4096,256]{1,0:T(8,128)} collective-permute-done((f32[4096,256]{1,0:T(8,128)}, f32[4096,256]{1,0:T(8,128)}, u32[]{:S(2)}, u32[]{:S(2)}) %collective-permute-start.1) | collective-permute-done | bytes 4194336 | tf_op jit(solution)/shard_map/ppermute | solution.py:11
  130.2 5.9 select_multiply_fusion.3
  136.1 1.6 collective-permute-start.2
  137.7 92.3 %collective-permute-done.2 = f32[4096,256]{1,0:T(8,128)} collective-permute-done((f32[4096,256]{1,0:T(8,128)}, f32[4096,256]{1,0:T(8,128)}, u32[]{:S(2)}, u32[]{:S(2)}) %collective-permute-start.2) | collective-permute-done | bytes 4194336 | tf_op jit(solution)/shard_map/ppermute | solution.py:11
  230.0 5.9 select_multiply_fusion.2
  236.0 2.4 collective-permute-start.3
  238.4 179.9 %collective-permute-done.3 = f32[4096,256]{1,0:T(8,128)} collective-permute-done((f32[4096,256]{1,0:T(8,128)}, f32[4096,256]{1,0:T(8,128)}, u32[]{:S(2)}, u32[]{:S(2)}) %collective-permute-start.3) | collective-permute-done | bytes 4194336 | tf_op jit(solution)/shard_map/ppermute | solution.py:11
  418.3 5.9 select_multiply_fusion.1
  424.2 6.0 collective-permute-start.4
  431.0 0.7 gather_fusion.1
  431.7 179.9 %collective-permute-done.4 = f32[4096,256]{1,0:T(8,128)} collective-permute-done((f32[4096,256]{1,0:T(8,128)}, f32[4096,256]{1,0:T(8,128)}, u32[]{:S(2)}, u32[]{:S(2)}) %collective-permute-start.4) | collective-permute-done | bytes 4194336 | tf_op jit(solution)/shard_map/ppermute | solution.py:11
  611.6 4.0 select_multiply_fusion
  615.6 4.4 fusion.4
  620.0 2.6 copy.6
  622.6 89.8 %reduce-scatter.2.cloned.1.call-done = f32[64,256]{1,0:T(8,128)} async-done(((f32[2048,256]{1,0:T(8,128)}), f32[64,256]{1,0:T(8,128)}) %reduce-scatter.2.cloned.1.call-update) | async-done | bytes 65552 | tf_op jit(solution)/shard_map/reduce_scatter | solution.py:74
  712.5 78.2 %all-reduce.2.cloned.1.call-done = f32[64,256]{1,0:T(8,128)} async-done(((f32[64,256]{1,0:T(8,128)}), f32[64,256]{1,0:T(8,128)}) %all-reduce.2.cloned.1.call-update) | async-done | bytes 65552 | tf_op jit(solution)/shard_map/psum | solution.py:75
  790.7 1.5 broadcast_multiply_fusion.1
  (14 shorter events, 0.8 us)
Async XLA Ops:
  6.5 423.7 %copy-start = (s32[32]{0:T(128)S(1)}, s32[32]{0:T(128)}, u32[]{:S(2)}) copy-start(s32[32]{0:T(128)} %param.8) | copy-start | bytes 388
  6.5 705.9 %reduce-scatter.2.cloned.1.call-start = ((), (), s32[]{:S(2)}) async-start(), calls=%async_computation.1 | async-start | bytes 2162688 | tf_op jit(solution)/shard_map/reduce_scatter | solution.py:74
  23.2 7.5 collective-permute-start
  36.7 93.5 %collective-permute-start.1 = (f32[4096,256]{1,0:T(8,128)}, f32[4096,256]{1,0:T(8,128)}, u32[]{:S(2)}, u32[]{:S(2)}) collective-permute-start(f32[4096,256]{1,0:T(8,128)} %select_multiply_fusion.4), channel_id=1, source_target_pairs={{0,2},{1,3},{2,0},{3,1},{4,6},{5,7},{6,4},{7,5},{8,10},{9,11},{10,... | collective-permute-start | bytes 12582920 | tf_op jit(solution)/shard_map/ppermute | solution.py:11
  136.1 93.9 %collective-permute-start.2 = (f32[4096,256]{1,0:T(8,128)}, f32[4096,256]{1,0:T(8,128)}, u32[]{:S(2)}, u32[]{:S(2)}) collective-permute-start(f32[4096,256]{1,0:T(8,128)} %select_multiply_fusion.3), channel_id=1, source_target_pairs={{0,4},{1,5},{2,6},{3,7},{4,0},{5,1},{6,2},{7,3},{8,12},{9,13},{10,... | collective-permute-start | bytes 12582920 | tf_op jit(solution)/shard_map/ppermute | solution.py:11
  236.0 182.3 %collective-permute-start.3 = (f32[4096,256]{1,0:T(8,128)}, f32[4096,256]{1,0:T(8,128)}, u32[]{:S(2)}, u32[]{:S(2)}) collective-permute-start(f32[4096,256]{1,0:T(8,128)} %select_multiply_fusion.2), channel_id=1, source_target_pairs={{0,8},{1,9},{2,10},{3,11},{4,12},{5,13},{6,14},{7,15},{8,0},{9,1},... | collective-permute-start | bytes 12582920 | tf_op jit(solution)/shard_map/ppermute | solution.py:11
  238.4 192.6 %copy-start.1 = (s32[32]{0:T(128)S(1)}, s32[32]{0:T(128)}, u32[]{:S(2)}) copy-start(s32[32]{0:T(128)} %param.9) | copy-start | bytes 388
  424.2 187.4 %collective-permute-start.4 = (f32[4096,256]{1,0:T(8,128)}, f32[4096,256]{1,0:T(8,128)}, u32[]{:S(2)}, u32[]{:S(2)}) collective-permute-start(f32[4096,256]{1,0:T(8,128)} %select_multiply_fusion.1), channel_id=1, source_target_pairs={{0,16},{1,17},{2,18},{3,19},{4,20},{5,21},{6,22},{7,23},{8,24},{9,... | collective-permute-start | bytes 12582920 | tf_op jit(solution)/shard_map/ppermute | solution.py:11
  622.6 168.1 %all-reduce.2.cloned.1.call-start = ((), (), s32[]{:S(2)}) async-start(), calls=%async_computation.2 | async-start | bytes 131072 | tf_op jit(solution)/shard_map/psum | solution.py:75
Sparse Core Ops, SparseCore 0:
  622.7 89.6 reduce-scatter.1
  715.0 75.5 all-reduce.1
where the time goes:
time: 799 us
  waiting for transfers between devices  719 us (90%)
  other arithmetic  32.6 us (4%)
  matrix products  17.8 us (2%)
  between operations  13.5 us (2%)
  starting transfers between devices  12.4 us (2%)
    ppermute x5, waiting for transfers between devices, swapped(): lax.ppermute(array, axis, [(i, i ^ 1 << stride) for i in range(lax.axis_s...  551 us
    reduce_scatter x1, waiting for transfers between devices, body(): lax.psum_scatter(partial_value, 'row', scatter_dimension=0, tiled=True)  89.8 us
    psum x1, waiting for transfers between devices, body(): summed = lax.psum(share, 'grp')  78.2 us
    mul x5, other arithmetic, body(): jnp.where(upper, partner - flipped, flipped + partner) * inverse_root  27.8 us
  transfers between devices with their start and end apart: 7, of which 7 were waited for; matrix products, arithmetic and copies ran while one was open for 0% of the time, Pallas kernels for 0%

commit v1 on v0

--- a/solution.py
+++ b/solution.py
@@ -72,7 +72,7 @@
     partial_value = partial_value.reshape(SKETCH, col_count)
     group_count = lax.axis_size("grp")
     share = lax.psum_scatter(partial_value, "row", scatter_dimension=0, tiled=True)
-    summed = lax.psum(share, "grp")
+    summed = jnp.sum(lax.all_gather(share, "grp"), axis=0)
     total_rows = row_count * dev_count * group_count
     return summed * math.sqrt(SKETCH / total_rows)
 

time: 799 us -> 750 us (0.939)
  waiting for transfers between devices: 719 us -> 641 us
  blocking collectives: 0 us -> 30.3 us
    psum x1 -> x0, waiting for transfers between devices: 78.2 us -> none  [body(): summed = lax.psum(share, 'grp')]
    all_gather x0 -> x1, blocking collectives: none -> 30.3 us  [body(): summed = jnp.sum(lax.all_gather(share, 'grp'), axis=0)]
  transfers between devices with their start and end apart: 7 -> 6, of which waited for: 7 -> 6; matrix products, arithmetic and copies ran while one was open for 0% -> 0% of each run, Pallas kernels for 0% -> 0%
where the time goes in v1:
time: 750 us
  waiting for transfers between devices  641 us (85%)
  other arithmetic  31.8 us (4%)
  blocking collectives  30.3 us (4%)
  matrix products  17.8 us (2%)
  between operations  13.5 us (2%)
  starting transfers between devices  12.3 us (2%)
    ppermute x5, waiting for transfers between devices, swapped(): lax.ppermute(array, axis, [(i, i ^ 1 << stride) for i in range(lax.axis_s...  551 us
    reduce_scatter x1, waiting for transfers between devices, body(): lax.psum_scatter(partial_value, 'row', scatter_dimension=0, tiled=True)  89.8 us
    all_gather x1, blocking collectives, body(): summed = jnp.sum(lax.all_gather(share, 'grp'), axis=0)  30.3 us
    mul x5, other arithmetic, body(): jnp.where(upper, partner - flipped, flipped + partner) * inverse_root  27.8 us
  transfers between devices with their start and end apart: 6, of which 6 were waited for; matrix products, arithmetic and copies ran while one was open for 0% of the time, Pallas kernels for 0%

profile of v1, /device:TPU:2, one launch (start us, length us, event | category | flops | bytes accessed | tf_op | source)
XLA Modules:
  0.0 750.2 jit_solution(14833899902822461225)
XLA Ops:
  6.5 0.7 convert_element_type.29
  7.3 2.6 broadcast_multiply_fusion
  9.9 6.3 fusion.2
  16.1 7.1 fusion.6
  23.2 7.5 collective-permute-done
  30.7 5.9 select_multiply_fusion.4
  36.7 2.3 collective-permute-start.1
  39.0 91.2 %collective-permute-done.1 = f32[4096,256]{1,0:T(8,128)} collective-permute-done((f32[4096,256]{1,0:T(8,128)}, f32[4096,256]{1,0:T(8,128)}, u32[]{:S(2)}, u32[]{:S(2)}) %collective-permute-start.1) | collective-permute-done | bytes 4194336 | tf_op jit(solution)/shard_map/ppermute | solution.py:11
  130.1 5.9 select_multiply_fusion.3
  136.1 1.6 collective-permute-start.2
  137.7 92.3 %collective-permute-done.2 = f32[4096,256]{1,0:T(8,128)} collective-permute-done((f32[4096,256]{1,0:T(8,128)}, f32[4096,256]{1,0:T(8,128)}, u32[]{:S(2)}, u32[]{:S(2)}) %collective-permute-start.2) | collective-permute-done | bytes 4194336 | tf_op jit(solution)/shard_map/ppermute | solution.py:11
  230.0 5.9 select_multiply_fusion.2
  235.9 2.4 collective-permute-start.3
  238.4 179.9 %collective-permute-done.3 = f32[4096,256]{1,0:T(8,128)} collective-permute-done((f32[4096,256]{1,0:T(8,128)}, f32[4096,256]{1,0:T(8,128)}, u32[]{:S(2)}, u32[]{:S(2)}) %collective-permute-start.3) | collective-permute-done | bytes 4194336 | tf_op jit(solution)/shard_map/ppermute | solution.py:11
  418.3 5.9 select_multiply_fusion.1
  424.2 6.0 collective-permute-start.4
  430.2 0.7 gather_fusion
  430.9 0.7 gather_fusion.1
  431.7 179.9 %collective-permute-done.4 = f32[4096,256]{1,0:T(8,128)} collective-permute-done((f32[4096,256]{1,0:T(8,128)}, f32[4096,256]{1,0:T(8,128)}, u32[]{:S(2)}, u32[]{:S(2)}) %collective-permute-start.4) | collective-permute-done | bytes 4194336 | tf_op jit(solution)/shard_map/ppermute | solution.py:11
  611.5 4.0 select_multiply_fusion
  615.6 4.4 fusion.4
  620.0 2.6 copy.6
  622.6 89.8 %reduce-scatter.2.cloned.1.call-done = f32[64,256]{1,0:T(8,128)} async-done(((f32[2048,256]{1,0:T(8,128)}), f32[64,256]{1,0:T(8,128)}) %reduce-scatter.2.cloned.1.call-update) | async-done | bytes 65552 | tf_op jit(solution)/shard_map/reduce_scatter | solution.py:74
  712.3 30.3 %all-gather = f32[512,256]{1,0:T(8,128)S(1)} all-gather(f32[64,256]{1,0:T(8,128)} %reduce-scatter.2.cloned.1.call-done), channel_id=2, replica_groups=mesh['grp'=8,'row'=32] {'grp'}, dimensions={0}, use_global_device_ids=true | all-gather | bytes 589824 | tf_op jit(solution)/shard_map/all_gather | solution.py:75
  (13 shorter events, 0.8 us)
Async XLA Ops:
  6.5 423.7 %copy-start = (s32[32]{0:T(128)S(1)}, s32[32]{0:T(128)}, u32[]{:S(2)}) copy-start(s32[32]{0:T(128)} %param.8) | copy-start | bytes 388
  6.5 705.8 %reduce-scatter.2.cloned.1.call-start = ((), (), s32[]{:S(2)}) async-start(), calls=%async_computation.1 | async-start | bytes 2162688 | tf_op jit(solution)/shard_map/reduce_scatter | solution.py:74
  23.2 7.5 %collective-permute-start = (f32[4096,256]{1,0:T(8,128)}, f32[4096,256]{1,0:T(8,128)}, u32[]{:S(2)}, u32[]{:S(2)}) collective-permute-start(f32[4096,256]{1,0:T(8,128)} %bitcast.10), channel_id=1, source_target_pairs={{0,1},{1,0},{2,3},{3,2},{4,5},{5,4},{6,7},{7,6},{8,9},{9,8},{10,11... | collective-permute-start | bytes 12582920 | tf_op jit(solution)/shard_map/ppermute | solution.py:11
  36.7 93.5 %collective-permute-start.1 = (f32[4096,256]{1,0:T(8,128)}, f32[4096,256]{1,0:T(8,128)}, u32[]{:S(2)}, u32[]{:S(2)}) collective-permute-start(f32[4096,256]{1,0:T(8,128)} %select_multiply_fusion.4), channel_id=1, source_target_pairs={{0,2},{1,3},{2,0},{3,1},{4,6},{5,7},{6,4},{7,5},{8,10},{9,11},{10,... | collective-permute-start | bytes 12582920 | tf_op jit(solution)/shard_map/ppermute | solution.py:11
  136.1 93.9 %collective-permute-start.2 = (f32[4096,256]{1,0:T(8,128)}, f32[4096,256]{1,0:T(8,128)}, u32[]{:S(2)}, u32[]{:S(2)}) collective-permute-start(f32[4096,256]{1,0:T(8,128)} %select_multiply_fusion.3), channel_id=1, source_target_pairs={{0,4},{1,5},{2,6},{3,7},{4,0},{5,1},{6,2},{7,3},{8,12},{9,13},{10,... | collective-permute-start | bytes 12582920 | tf_op jit(solution)/shard_map/ppermute | solution.py:11
  235.9 182.3 %collective-permute-start.3 = (f32[4096,256]{1,0:T(8,128)}, f32[4096,256]{1,0:T(8,128)}, u32[]{:S(2)}, u32[]{:S(2)}) collective-permute-start(f32[4096,256]{1,0:T(8,128)} %select_multiply_fusion.2), channel_id=1, source_target_pairs={{0,8},{1,9},{2,10},{3,11},{4,12},{5,13},{6,14},{7,15},{8,0},{9,1},... | collective-permute-start | bytes 12582920 | tf_op jit(solution)/shard_map/ppermute | solution.py:11
  238.4 192.6 %copy-start.1 = (s32[32]{0:T(128)S(1)}, s32[32]{0:T(128)}, u32[]{:S(2)}) copy-start(s32[32]{0:T(128)} %param.9) | copy-start | bytes 388
  424.2 187.4 %collective-permute-start.4 = (f32[4096,256]{1,0:T(8,128)}, f32[4096,256]{1,0:T(8,128)}, u32[]{:S(2)}, u32[]{:S(2)}) collective-permute-start(f32[4096,256]{1,0:T(8,128)} %select_multiply_fusion.1), channel_id=1, source_target_pairs={{0,16},{1,17},{2,18},{3,19},{4,20},{5,21},{6,22},{7,23},{8,24},{9,... | collective-permute-start | bytes 12582920 | tf_op jit(solution)/shard_map/ppermute | solution.py:11
Sparse Core Ops, SparseCore 0:
  622.7 89.6 reduce-scatter.1
